TPU v7x, 512 devices: a whole 4x4x16 slice. The times are simulated.
512 devices in a mesh: grp: 16 (over z_lo, x), fsdp: 4 (over y), tp: 8 (over z_hi, core).
Axes of the slice: x: 4, y: 4, z: 16 (z_hi: 4, z_lo: 4; z = z_hi * 4 + z_lo), core: 2. Of those that a mesh axis runs over, the one named last changes fastest.
Arguments:
- frames: bfloat16 [3072, 5120], P('fsdp', 'grp'), may hold values from -6 to 6
- projector: bfloat16 [5120, 8192], P('grp', 'tp'), may hold values from -0.078125 to 0.078125
- text_token_embedding: bfloat16 [16384, 8192], P(('grp', 'fsdp'), 'tp'), may hold values from -6 to 6
- norm_gain_vector: float32 [8192], replicated, may hold values from 0.1 to 1.9
- frozen: bfloat16 [8192, 1024], P('fsdp', 'tp'), may hold values from -0.0625 to 0.0625
- adapter_down_map: bfloat16 [8192, 64], P('fsdp'), may hold values from -0.0625 to 0.0625
- adapter_up_map: bfloat16 [64, 1024], P(None, 'tp'), may hold values from -0.75 to 0.75
- clip_frame_length: int32 [4, 16, 16], P('fsdp'), may hold values from 1 to 6, as said below
- audio_first_token: int32 [4, 16, 16], P('fsdp'), may hold values from 0 to 255, as said below
- segment_document_index: int32 [16384], P(('grp', 'fsdp')), may hold values from 0 to 255, never falling along the last dimension, each value on 1 to 256 neighbouring positions
- keep_document_flags: int32 [256], replicated, may hold values 0 or 1
- cotangent: bfloat16 [16384, 1024], P(('grp', 'fsdp'), 'tp'), may hold values from -0.046875 to 0.046875
Outputs:
- value_output: bfloat16 [16384, 1024], P(('grp', 'fsdp'), 'tp')
- projector_grad: float32 [5120, 8192], P('grp', 'tp')
- down_map_gradient: float32 [8192, 64], P('tp')
- up_map_gradient: float32 [64, 1024], P(None, 'tp')
Inputs may be any that keep to these rules, and one draw needn't show every extreme that they name: `clip_frame_length`: entry [f, g, k] is the length of clip k of frame block f * 16 + g; the 16 clips of a block sum to 48, and one of them has exactly 6 frames. `audio_first_token`: entry [f, g, k] is the first token, among the 256 tokens of block k * 4 + f, of the audio slots of clip k of frame block f * 16 + g; the 16 clips that one token block takes lie in distinct aligned windows of 16 tokens.
All inputs are finite; a program needn't handle non-finite values.
Results may differ from a plain program's by a relative error of at most 0.018.
Values may be sent and summed in bfloat16 or wider, within the bound.
No kernel may reach another device: no remote copies, remote signals or barrier semaphores. Data moves between devices by JAX's collectives and lax.ppermute only.
A program may use at most 128 MiB of HBM per device.

v0:
```python
import jax
import jax.numpy as jnp
from jax import lax
from jax.sharding import Mesh, PartitionSpec as P

adapter_scale = 2.0
norm_eps = 1e-05
GRP = ("zl", "x")
TP = ("zh", "c")
bf16, f32 = (jnp.bfloat16, jnp.float32)


def dot(a, b, ca, cb):
    return lax.dot_general(a, b, (((ca,), (cb,)), ((), ())), preferred_element_type=f32)


def exchange(blocks, axis):
    return lax.all_to_all(blocks, axis, split_axis=0, concat_axis=0, tiled=True)


def pick_entry(grid_in, position, which_axis):
    matches = lax.broadcasted_iota(jnp.int32, grid_in.shape, which_axis) == position
    return jnp.sum(jnp.where(matches, grid_in, 0), axis=which_axis)


def after(x, other):
    return x + (other[(0,) * other.ndim] * 0).astype(x.dtype)


def copies(x, n):
    return jnp.broadcast_to(x[None], (n, *x.shape))


def two_halves(v):
    hi = lax.reduce_precision(v, 8, 7)
    return (hi.astype(bf16), (v - hi).astype(bf16))


def shards(
    frames,
    projector,
    text,
    gain_all,
    frozen,
    down,
    up,
    clip_len,
    first_token,
    segment,
    keep,
    cotangent,
):
    nx, ny, nzl, ng, nt = (lax.axis_size(a) for a in ("x", "y", "zl", GRP, TP))
    grp_index, tp_index = (lax.axis_index(GRP), lax.axis_index(TP))
    x_index, y_index = (lax.axis_index("x"), lax.axis_index("y"))
    toks, width = text.shape
    cols, rank = (frozen.shape[1], down.shape[1])
    n_frames = frames.shape[0] // ng
    full_width = width * nt
    cap = 2 * n_frames // ng
    slots = ng * cap
    rows = toks + n_frames
    gain = lax.dynamic_slice_in_dim(gain_all, tp_index * width, width, 0)
    by_x = jnp.moveaxis(frames.reshape(nzl, nx, n_frames, frames.shape[1]), 1, 0)
    partial = dot(by_x.reshape(frames.shape), projector, 1, 0).astype(bf16)
    x_sum = lax.psum_scatter(partial, "x", scatter_dimension=0, tiled=True)
    all_frames = lax.all_gather(by_x.reshape(frames.shape), "y", axis=0, tiled=True)
    own_sizes = pick_entry(clip_len[0], grp_index, 0)
    before = lax.broadcasted_iota(jnp.int32, (ng, ng), 1) < lax.broadcasted_iota(
        jnp.int32, (ng, ng), 0
    )
    own_starts = jnp.sum(jnp.where(before, own_sizes[None, :], 0), axis=1)
    slot_offset = lax.broadcasted_iota(jnp.int32, (ng, cap), 1)
    frame_slot = own_starts[:, None] + slot_offset
    slot_live = slot_offset < own_sizes[:, None]
    frame_iota = lax.broadcasted_iota(jnp.int32, (ng, cap, n_frames), 2)
    sender = (
        ((frame_iota == frame_slot[:, :, None]) & slot_live[:, :, None])
        .astype(bf16)
        .reshape(slots, n_frames)
    )
    in_sizes = pick_entry(clip_len[0], grp_index, 1)
    arrive_at = pick_entry(first_token[0], grp_index, 1)
    token_iota = lax.broadcasted_iota(jnp.int32, (toks, ng, cap), 0)
    receive_mask = (token_iota == (arrive_at[:, None] + slot_offset)[None]) & (
        slot_offset < in_sizes[:, None]
    )[None]
    receiver = receive_mask.astype(bf16).reshape(toks, slots)
    is_audio = jnp.any(receive_mask, axis=(1, 2))
    doc_iota = lax.broadcasted_iota(jnp.int32, (toks, keep.shape[0]), 1)
    kept = jnp.sum(jnp.where(segment[:, None] == doc_iota, keep[None, :], 0), axis=1)
    grad_tok = cotangent * kept.astype(bf16)[:, None]
    grad_slots = exchange(dot(receiver, grad_tok, 0, 0).astype(bf16).reshape(ng, cap, cols), GRP)
    grad_frames = dot(sender, grad_slots.reshape(slots, cols), 0, 0).astype(bf16)
    grad_text = jnp.where(is_audio[:, None], jnp.zeros_like(grad_tok), grad_tok)
    grad_rows = jnp.concatenate([grad_text, grad_frames], axis=0)
    piece = width // (ny * nx)
    w_piece = lax.dynamic_index_in_dim(frozen.reshape(2, ny, nx, piece, cols), x_index, 2, False)
    down_half = lax.dynamic_slice_in_dim(down.T, lax.rem(tp_index, 2) * width, width, 1)
    down_half = jnp.moveaxis(down_half.reshape(rank, nt, cols), 1, 0).reshape(nt * rank, cols)

    def for_y(k):
        w = lax.dynamic_index_in_dim(w_piece, lax.rem(y_index + k, ny), 1, False)
        return jnp.concatenate([w.reshape(2 * piece, cols), down_half], axis=0)

    y_parts = [for_y(0)] + [
        lax.ppermute(for_y(k), "y", [(i, (i + k) % ny) for i in range(ny)]) for k in range(1, ny)
    ]
    y_parts = jnp.stack([lax.select_n(lax.rem(y_index - j + ny, ny), *y_parts) for j in range(ny)])
    wa = y_parts[:, : 2 * piece].reshape(nt, piece, cols)
    down_t = lax.dynamic_index_in_dim(y_parts[:, 2 * piece :], tp_index // 2, 0, False)
    down_t = jnp.moveaxis(down_t.reshape(nt, rank, cols), 0, 1).reshape(rank, width)
    up_rows = rank // nx
    up_piece = lax.dynamic_slice_in_dim(up, x_index * up_rows, up_rows, 0)
    text_wide = text.astype(f32)
    text_scaled = text_wide * gain[None, :]
    pair = jnp.concatenate(
        [
            (adapter_scale * dot(grad_text, up, 1, 1)).astype(bf16),
            dot(text_scaled.astype(bf16), down_t, 1, 1).astype(bf16),
        ],
        axis=1,
    )
    sq_text = dot(jnp.ones((8, width), bf16), (text_wide * text_wide).astype(bf16), 1, 1)[0]
    sent = jnp.concatenate(
        [
            wa,
            copies(jnp.concatenate([up_piece, grad_frames], axis=0), nt),
            pair.reshape(nt, toks // nt, cols),
        ],
        axis=1,
    )
    came = exchange(sent, TP)
    at = piece + up_rows
    pair = jnp.sum(came[:, at + n_frames :].astype(f32), axis=0).astype(bf16)
    blocks = exchange(x_sum.reshape(nzl, n_frames, width), "zl")
    embedded = jnp.sum(blocks.astype(f32), axis=0).astype(bf16)
    wide = embedded.astype(f32)
    scaled = wide * gain[None, :]
    grad_full = jnp.moveaxis(came[:, at : at + n_frames], 0, 1).reshape(n_frames, nt * cols)
    grad_all = lax.all_gather(grad_full, "y", axis=0, tiled=True)
    weights = jnp.moveaxis(came[:, :at], 0, 1).reshape(at, nt * cols)
    weights = lax.all_gather(weights, "x")
    up_full = weights[:, piece:].reshape(rank, nt * cols)
    weights = weights[:, :piece].reshape(nx * piece, nt * cols)
    lora_frames = (adapter_scale * dot(grad_full, up_full, 1, 1)).astype(bf16)
    spread = dot(grad_all, weights, 1, 1).astype(bf16).reshape(ny, n_frames, nx * piece)
    back = jnp.moveaxis(exchange(after(spread, embedded), "y"), 0, 1)
    grad_norm = back.reshape(n_frames, width).astype(f32)
    grad_norm = grad_norm + dot(lora_frames, down_t, 1, 0)
    weights = lax.all_gather(weights, "y", axis=0, tiled=True)
    sq_hi, sq_lo = two_halves(jnp.sum(wide * wide, axis=1, keepdims=True))
    d_hi, d_lo = two_halves(jnp.sum(scaled * grad_norm, axis=1, keepdims=True))
    low_frames = dot(scaled.astype(bf16), down_t, 1, 1).astype(bf16)
    spare = jnp.zeros((n_frames, cols - rank - 4), bf16)
    of_frames = jnp.concatenate([low_frames, sq_hi, sq_lo, d_hi, d_lo, spare], axis=1)
    n_l = toks // cols
    t_hi, t_lo = two_halves(sq_text.reshape(n_l, cols))
    spare = jnp.zeros((8 - 2 * n_l, cols), bf16)
    stats = jnp.concatenate([of_frames, t_hi, t_lo, spare, pair], axis=0)
    stats = exchange(copies(stats, nt), TP)
    pair = stats[:, n_frames + 8 :].reshape(toks, cols)
    stats = jnp.sum(stats[:, : n_frames + 8].astype(f32), axis=0)
    sq_frames = stats[:n_frames, rank : rank + 1] + stats[:n_frames, rank + 1 : rank + 2]
    dots = stats[:n_frames, rank + 2 : rank + 3] + stats[:n_frames, rank + 3 : rank + 4]
    sq_text = (
        stats[n_frames : n_frames + n_l] + stats[n_frames + n_l : n_frames + 2 * n_l]
    ).reshape(toks, 1)
    inv_rms = lax.rsqrt(jnp.concatenate([sq_text, sq_frames], axis=0) / full_width + norm_eps)
    lora = jnp.concatenate([pair[:, :rank], lora_frames], axis=0)
    low = jnp.concatenate([pair[:, rank:].astype(f32), stats[:n_frames, :rank]], axis=0)
    low_half = (low * inv_rms).astype(bf16)
    all_scaled = jnp.concatenate([text_scaled, scaled], axis=0)
    base = dot(all_scaled.astype(bf16), weights, 1, 0).astype(bf16)
    base = jnp.moveaxis(base.reshape(rows, nt, cols), 1, 0).reshape(nt * rows, cols)
    summed = lax.psum_scatter(base, TP, scatter_dimension=0, tiled=True)
    normed = (all_scaled * inv_rms).astype(bf16)
    quarter = width // ny
    down_part = dot(lora, normed, 0, 0).astype(bf16).reshape(nzl, ny * nx, width)
    up_part = (adapter_scale * dot(low_half, grad_rows, 0, 0)).astype(bf16)
    up_part = jnp.pad(up_part, ((0, 0), (0, width - cols))).reshape(nzl, ny * nx, width)
    adapters = jnp.concatenate([down_part, up_part], axis=1)
    inv_f = after(inv_rms[toks:], base)
    frame_grad = (
        inv_f * gain[None, :] * grad_norm - wide * (inv_f * inv_f * inv_f * dots / full_width)
    ).astype(bf16)
    came = exchange(jnp.concatenate([copies(frame_grad, nzl), adapters], axis=1), "zl")
    adapters = jnp.sum(came[:, n_frames:].astype(f32), axis=0).astype(bf16)
    frame_grad = came[:, :n_frames]
    n_x = nzl * n_frames
    frame_grad = jnp.moveaxis(frame_grad.reshape(n_x, ny, quarter), 1, 0)
    frame_grad = jnp.broadcast_to(frame_grad[:, None], (ny, nx, n_x, quarter))
    frame_grad = frame_grad.reshape(ny * nx, n_x, quarter)
    down_part = adapters[: ny * nx].reshape(ny * nx, ny, quarter)
    up_part = adapters[ny * nx :, :quarter].reshape(ny * nx, 1, quarter)
    spare = jnp.zeros((ny * nx, 7 - ny, quarter), bf16)
    came = exchange(jnp.concatenate([frame_grad, down_part, up_part, spare], axis=1), ("y", "x"))
    own = jnp.sum(came[:, n_x : n_x + ny + 1].astype(f32), axis=0).astype(bf16)
    own = jnp.concatenate([own[:ny].reshape(width // cols, cols), own[ny:, :cols]], axis=0)
    values = summed.astype(f32) * inv_rms + adapter_scale * dot(low_half, up, 1, 0)
    values = values.astype(bf16)
    out_slots = dot(sender, values[toks:], 1, 0).astype(bf16).reshape(nzl, 1, nx, cap, cols)
    out_slots = jnp.broadcast_to(out_slots, (nzl, ny, nx, cap, cols)).reshape(ny * ng, cap, cols)
    last = exchange(jnp.concatenate([copies(own, ny * ng), out_slots], axis=1), ("zl", "y", "x"))
    n_d = width // cols
    down_grad = last[:, :n_d].reshape(rank, width).astype(f32).T
    up_grad = last[:, n_d].astype(f32)
    all_grad = came[:, :n_x].reshape(ny * nx * n_x, quarter)
    projector_grad = after(dot(all_frames, all_grad, 0, 0), summed).astype(bf16)
    projector_grad = lax.all_gather(projector_grad, "y", axis=1, tiled=True).astype(f32)
    in_slots = last[:, -cap:].reshape(nzl, ny, nx * cap, cols)
    in_slots = lax.dynamic_index_in_dim(in_slots, y_index, 1, False).reshape(slots, cols)
    audio_values = dot(receiver, in_slots, 1, 0).astype(bf16)
    value_output = jnp.where(is_audio[:, None], audio_values, values[:toks])
    return (value_output, projector_grad, down_grad, up_grad)


def solution(mesh):
    sizes = dict(zip(mesh.axis_names, mesh.devices.shape))
    half = sizes["grp"] // 4
    mesh = Mesh(
        mesh.devices.reshape(half, 4, sizes["fsdp"], sizes["tp"] // 2, 2),
        ("zl", "x", "y", "zh", "c"),
    )
    rows = ("zl", "x", "y")
    in_specs = (
        P("y", GRP),
        P(GRP, TP),
        P(rows, TP),
        P(),
        P("y", TP),
        P("y", None),
        P(None, TP),
        P("y", None, None),
        P("y", None, None),
        P(rows),
        P(),
        P(rows, TP),
    )
    out_specs = (P(rows, TP), P(GRP, TP), P(TP, None), P(None, TP))
    return jax.shard_map(shards, mesh=mesh, in_specs=in_specs, out_specs=out_specs, check_vma=False)
```

profile of v0, /device:TPU:2, one launch (start us, length us, event | category | flops | bytes accessed | tf_op | source)
XLA Modules:
  0.0 244.0 jit_solution(16889027735061551922)
XLA Ops:
  8.1 1.1 dynamic-slice_bitcast_fusion
  9.2 0.8 constant_dynamic-slice_fusion.6
  10.1 5.1 %collective-permute-start.1 = (bf16[640,128]{1,0:T(8,128)(2,1)S(1)}, bf16[640,128]{1,0:T(8,128)(2,1)S(1)}, u32[]{:S(2)}, u32[]{:S(2)}) collective-permute-start(bf16[640,128]{1,0:T(8,128)(2,1)S(1)} %get-tuple-element.21), channel_id=1, source_target_pairs={{0,16},{8,24},{16,0},{24,8},{1,17},{9,25},{17,1},{25,9},{2,18},{10... | collective-permute-start | bytes 491528 | tf_op jit(solution)/shard_map/ppermute | solution.py:107
  15.2 3.0 %collective-permute-start.2 = (bf16[640,128]{1,0:T(8,128)(2,1)S(1)}, bf16[640,128]{1,0:T(8,128)(2,1)S(1)}, u32[]{:S(2)}, u32[]{:S(2)}) collective-permute-start(bf16[640,128]{1,0:T(8,128)(2,1)S(1)} %get-tuple-element.22), channel_id=1, source_target_pairs={{0,24},{8,0},{16,8},{24,16},{1,25},{9,1},{17,9},{25,17},{2,26},{10... | collective-permute-start | bytes 491528 | tf_op jit(solution)/shard_map/ppermute | solution.py:107
  18.2 2.9 %collective-permute-start = (bf16[640,128]{1,0:T(8,128)(2,1)S(1)}, bf16[640,128]{1,0:T(8,128)(2,1)S(1)}, u32[]{:S(2)}, u32[]{:S(2)}) collective-permute-start(bf16[640,128]{1,0:T(8,128)(2,1)S(1)} %get-tuple-element.20), channel_id=1, source_target_pairs={{0,8},{8,16},{16,24},{24,0},{1,9},{9,17},{17,25},{25,1},{2,10},{10... | collective-permute-start | bytes 491528 | tf_op jit(solution)/shard_map/ppermute | solution.py:107
  22.4 0.5 fusion.73
  23.2 0.6 reshape.404
  23.8 8.9 %all-to-all-start.1 = ((bf16[16,6,128]{2,1,0:T(8,128)(2,1)}), bf16[16,6,128]{2,1,0:T(8,128)(2,1)S(1)}, u32[]{:S(2)}, u32[]{:S(2)}) async-start(bf16[16,6,128]{2,1,0:T(8,128)(2,1)} %reshape.404), calls=%async_computation.2 | async-start | bytes 65536 | tf_op jit(solution)/shard_map/all_to_all | solution.py:18
  32.8 0.3 copy.181
  33.2 2.1 convolution_convert_fusion
  36.1 0.7 dynamic_slice.32
  36.9 2.5 %all-to-all-done.1 = bf16[16,6,128]{2,1,0:T(8,128)(2,1)S(1)} async-done(((bf16[16,6,128]{2,1,0:T(8,128)(2,1)}), bf16[16,6,128]{2,1,0:T(8,128)(2,1)S(1)}, u32[]{:S(2)}, u32[]{:S(2)}) %all-to-all-start.1) | async-done | bytes 24608 | tf_op jit(solution)/shard_map/all_to_all | solution.py:18
  40.4 0.5 copy-done.4
  41.4 35.7 %all_to_all.40 = bf16[8,160,128]{2,1,0:T(8,128)(2,1)S(1)} all-to-all(bf16[8,160,128]{2,1,0:T(8,128)(2,1)S(1)} %pad_maximum_fusion.3), channel_id=1, replica_groups=mesh['zl'=4,'x'=4,'y'=4,'zh'=4,'c'=2] {'zh','c'}, dimensions={0} | all-to-all | bytes 655360 | tf_op jit(solution)/shard_map/all_to_all | solution.py:18
  77.3 11.8 %all_gather.16 = bf16[4,80,1024]{2,1,0:T(8,128)(2,1)S(1)} all-gather(bf16[1,80,1024]{2,1,0:T(8,128)(2,1)S(1)} %all_gather_reshape.3), channel_id=1, replica_groups=mesh['zl'=4,'x'=4,'y'=4,'zh'=4,'c'=2] {'x'}, dimensions={0}, use_global_device_ids=true | all-gather | bytes 819200 | tf_op jit(solution)/shard_map/all_gather | solution.py:143
  89.2 0.8 slice.149
  90.0 5.7 %all-to-all-start = ((bf16[4,48,1024]{2,1,0:T(8,128)(2,1)}), bf16[4,48,1024]{2,1,0:T(8,128)(2,1)S(1)}, u32[]{:S(2)}, u32[]{:S(2)}) async-start(bf16[4,48,1024]{2,1,0:T(8,128)(2,1)} %bitcast.171), calls=%async_computation.1 | async-start | bytes 786432 | tf_op jit(solution)/shard_map/all_to_all | solution.py:18
  96.0 13.7 %all_gather.15 = bf16[192,1024]{1,0:T(8,128)(2,1)S(1)} all-gather(bf16[48,1024]{1,0:T(8,128)(2,1)S(1)} %copy_bitcast_fusion.1), channel_id=1, replica_groups=mesh['zl'=4,'x'=4,'y'=4,'zh'=4,'c'=2] {'y'}, dimensions={0}, use_global_device_ids=true | all-gather | bytes 491520 | tf_op jit(solution)/shard_map/all_gather | solution.py:141
  109.9 0.5 slice.150
  111.1 1.0 fusion.5
  112.1 3.5 %all-to-all-start.3 = ((bf16[4,48,256]{2,1,0:T(8,128)(2,1)}), bf16[4,48,256]{2,1,0:T(8,128)(2,1)S(1)}, u32[]{:S(2)}, u32[]{:S(2)}) async-start(bf16[4,48,256]{2,1,0:T(8,128)(2,1)} %bitcast.28), calls=%async_computation.4 | async-start | bytes 196608 | tf_op jit(solution)/shard_map/all_to_all | solution.py:18
  115.7 6.7 %all-to-all-done.3 = bf16[4,48,256]{2,1,0:T(8,128)(2,1)S(1)} async-done(((bf16[4,48,256]{2,1,0:T(8,128)(2,1)}), bf16[4,48,256]{2,1,0:T(8,128)(2,1)S(1)}, u32[]{:S(2)}, u32[]{:S(2)}) %all-to-all-start.3) | async-done | bytes 98336 | tf_op jit(solution)/shard_map/all_to_all | solution.py:18
  123.3 0.7 broadcast_in_dim.120
  124.0 3.4 %all-to-all-start.4 = ((bf16[8,88,128]{2,1,0:T(8,128)(2,1)}), bf16[8,88,128]{2,1,0:T(8,128)(2,1)S(1)}, u32[]{:S(2)}, u32[]{:S(2)}) async-start(bf16[8,88,128]{2,1,0:T(8,128)(2,1)} %broadcast_in_dim.120), calls=%async_computation.5 | async-start | bytes 360448 | tf_op jit(solution)/shard_map/all_to_all | solution.py:18
  127.6 2.4 fusion
  130.1 0.6 slice.158
  131.4 15.7 %all-to-all-done.4 = bf16[8,88,128]{2,1,0:T(8,128)(2,1)S(1)} async-done(((bf16[8,88,128]{2,1,0:T(8,128)(2,1)}), bf16[8,88,128]{2,1,0:T(8,128)(2,1)S(1)}, u32[]{:S(2)}, u32[]{:S(2)}) %all-to-all-start.4) | async-done | bytes 180256 | tf_op jit(solution)/shard_map/all_to_all | solution.py:18
  147.7 0.3 convolution_convert_fusion.2
  148.5 0.9 pad_maximum_fusion.2
  149.3 3.6 %all-to-all-start.5 = ((bf16[4,80,1024]{2,1,0:T(8,128)(2,1)}), bf16[4,80,1024]{2,1,0:T(8,128)(2,1)S(1)}, u32[]{:S(2)}, u32[]{:S(2)}) async-start(bf16[4,80,1024]{2,1,0:T(8,128)(2,1)} %pad_maximum_fusion.2), calls=%async_computation.6 | async-start | bytes 1310720 | tf_op jit(solution)/shard_map/all_to_all | solution.py:18
  153.0 0.7 reduce-scatter.5.cloned.1.call-update
  153.8 0.5 all-gather.5.cloned.1.call-update
  154.4 16.3 %all-to-all-done.5 = bf16[4,80,1024]{2,1,0:T(8,128)(2,1)S(1)} async-done(((bf16[4,80,1024]{2,1,0:T(8,128)(2,1)}), bf16[4,80,1024]{2,1,0:T(8,128)(2,1)S(1)}, u32[]{:S(2)}, u32[]{:S(2)}) %all-to-all-start.5) | async-done | bytes 655392 | tf_op jit(solution)/shard_map/all_to_all | solution.py:18
  171.3 1.8 maximum_maximum_fusion
  173.2 6.0 %all-to-all-start.6 = ((bf16[16,200,256]{2,1,0:T(8,128)(2,1)}), bf16[16,200,256]{2,1,0:T(8,128)(2,1)S(1)}, u32[]{:S(2)}, u32[]{:S(2)}) async-start(bf16[16,200,256]{2,1,0:T(8,128)(2,1)} %maximum_maximum_fusion), calls=%async_computation.7 | async-start | bytes 3276800 | tf_op jit(solution)/shard_map/all_to_all | solution.py:18
  179.1 22.8 %reduce-scatter.5.cloned.1.call-done = bf16[304,128]{1,0:T(8,128)(2,1)} async-done(((bf16[2432,128]{1,0:T(8,128)(2,1)}), bf16[304,128]{1,0:T(8,128)(2,1)}) %reduce-scatter.5.cloned.1.call-update) | async-done | bytes 77840 | tf_op jit(solution)/shard_map/reduce_scatter | solution.py:176
  202.0 1.1 fusion.4
  203.3 0.9 all-to-all-done.6
  204.4 0.8 pad_maximum_fusion.4
  205.2 7.2 %all-to-all-start.7 = ((bf16[64,15,128]{2,1,0:T(8,128)(2,1)}), bf16[64,15,128]{2,1,0:T(8,128)(2,1)S(1)}, u32[]{:S(2)}, u32[]{:S(2)}) async-start(bf16[64,15,128]{2,1,0:T(8,128)(2,1)} %pad_maximum_fusion.4), calls=%async_computation.9 | async-start | bytes 524288 | tf_op jit(solution)/shard_map/all_to_all | solution.py:18
  212.4 1.2 slice.176
  214.2 1.3 slice.175
  215.5 3.1 %fusion.2 = bf16[320,256]{1,0:T(8,128)(2,1)S(1)} fusion(bf16[3072,256]{1,0:T(8,128)(2,1)} %bitcast.158, bf16[3072,320]{1,0:T(8,128)(2,1)} %all-gather.5.cloned.1.call-done, f32[]{:T(128)S(6)} %convert.12), kind=kOutput, calls=%fused_computation.12 | convolution fusion | flops 503480320 | bytes 3702788 | tf_op jit(solution)/shard_map/dot_general | solution.py:14
  218.7 14.4 %all_gather.19 = bf16[320,1024]{1,0:T(8,128)(2,1)S(1)} all-gather(bf16[320,256]{1,0:T(8,128)(2,1)S(1)} %fusion.2), channel_id=1, replica_groups=mesh['zl'=4,'x'=4,'y'=4,'zh'=4,'c'=2] {'y'}, dimensions={1}, use_global_device_ids=true | all-gather | bytes 819200 | tf_op jit(solution)/shard_map/all_gather | solution.py:210
  233.0 1.2 convert_element_type.229
  234.4 0.8 copy.243
  235.1 0.9 fusion.6
  236.0 0.6 slice_convert_fusion.2
  (153 shorter events, 8.1 us)
Async XLA Ops:
  8.0 25.1 %copy-start = (bf16[320,1024]{1,0:T(8,128)(2,1)S(1)}, bf16[320,1024]{1,0:T(8,128)(2,1)}, u32[]{:S(2)}) copy-start(bf16[320,1024]{1,0:T(8,128)(2,1)} %param.13) | copy-start | bytes 1966084
  8.0 13.1 %copy-start.10 = (s32[1,16,16]{2,1,0:T(8,128)S(1)}, s32[1,16,16]{2,1,0:T(8,128)}, u32[]{:S(2)}) copy-start(s32[1,16,16]{2,1,0:T(8,128)} %param.19) | copy-start | bytes 3076
  8.0 13.1 %copy-start.11 = (s32[1,16,16]{2,1,0:T(8,128)S(1)}, s32[1,16,16]{2,1,0:T(8,128)}, u32[]{:S(2)}) copy-start(s32[1,16,16]{2,1,0:T(8,128)} %param.20) | copy-start | bytes 3076
  8.0 14.1 %copy-start.12 = (s32[256]{0:T(256)S(1)}, s32[256]{0:T(256)}, u32[]{:S(2)}) copy-start(s32[256]{0:T(256)} %param.22) | copy-start | bytes 3076
  8.0 14.1 %copy-start.13 = (s32[256]{0:T(256)S(1)}, s32[256]{0:T(256)}, u32[]{:S(2)}) copy-start(s32[256]{0:T(256)} %param.21) | copy-start | bytes 3076
  8.1 14.8 %copy-start.6 = (bf16[256,128]{1,0:T(8,128)(2,1)S(1)}, bf16[256,128]{1,0:T(8,128)(2,1)}, u32[]{:S(2)}) copy-start(bf16[256,128]{1,0:T(8,128)(2,1)} %param.23) | copy-start | bytes 196612
  8.1 24.7 %copy-start.5 = (bf16[768,320]{0,1:T(8,128)(2,1)S(1)}, bf16[768,320]{0,1:T(8,128)(2,1)}, u32[]{:S(2)}) copy-start(bf16[768,320]{0,1:T(8,128)(2,1)} %param.12) | copy-start | bytes 1474564
  10.1 29.6 %collective-permute-start.1 = (bf16[640,128]{1,0:T(8,128)(2,1)S(1)}, bf16[640,128]{1,0:T(8,128)(2,1)S(1)}, u32[]{:S(2)}, u32[]{:S(2)}) collective-permute-start(bf16[640,128]{1,0:T(8,128)(2,1)S(1)} %get-tuple-element.21), channel_id=1, source_target_pairs={{0,16},{8,24},{16,0},{24,8},{1,17},{9,25},{17,1},{25,9},{2,18},{10... | collective-permute-start | bytes 491528 | tf_op jit(solution)/shard_map/ppermute | solution.py:107
  15.2 24.5 %collective-permute-start.2 = (bf16[640,128]{1,0:T(8,128)(2,1)S(1)}, bf16[640,128]{1,0:T(8,128)(2,1)S(1)}, u32[]{:S(2)}, u32[]{:S(2)}) collective-permute-start(bf16[640,128]{1,0:T(8,128)(2,1)S(1)} %get-tuple-element.22), channel_id=1, source_target_pairs={{0,24},{8,0},{16,8},{24,16},{1,25},{9,1},{17,9},{25,17},{2,26},{10... | collective-permute-start | bytes 491528 | tf_op jit(solution)/shard_map/ppermute | solution.py:107
  18.2 21.6 %collective-permute-start = (bf16[640,128]{1,0:T(8,128)(2,1)S(1)}, bf16[640,128]{1,0:T(8,128)(2,1)S(1)}, u32[]{:S(2)}, u32[]{:S(2)}) collective-permute-start(bf16[640,128]{1,0:T(8,128)(2,1)S(1)} %get-tuple-element.20), channel_id=1, source_target_pairs={{0,8},{8,16},{16,24},{24,0},{1,9},{9,17},{17,25},{25,1},{2,10},{10... | collective-permute-start | bytes 491528 | tf_op jit(solution)/shard_map/ppermute | solution.py:107
  23.8 15.7 %all-to-all-start.1 = ((bf16[16,6,128]{2,1,0:T(8,128)(2,1)}), bf16[16,6,128]{2,1,0:T(8,128)(2,1)S(1)}, u32[]{:S(2)}, u32[]{:S(2)}) async-start(bf16[16,6,128]{2,1,0:T(8,128)(2,1)} %reshape.404), calls=%async_computation.2 | async-start | bytes 65536 | tf_op jit(solution)/shard_map/all_to_all | solution.py:18
  32.7 57.3 %reduce-scatter.3.cloned.1.call-start = ((), (), s32[]{:S(2)}) async-start(), calls=%async_computation.10 | async-start | bytes 1966080 | tf_op jit(solution)/shard_map/reduce_scatter | solution.py:66
  33.1 2.2 copy-start.3
  35.3 1.5 copy-start.7
  35.3 92.3 %all-gather.3.cloned.1.call-start = ((), (), s32[]{:S(2)}) async-start(), calls=%async_computation.11 | async-start | bytes 2621440 | tf_op jit(solution)/shard_map/all_gather | solution.py:151
  39.7 0.6 copy-start.8
  39.9 1.0 copy-start.4
  90.0 21.1 %copy-start.1 = (bf16[4,64,1024]{2,1,0:T(8,128)(2,1)S(1)}, bf16[4,64,1024]{2,1,0:T(8,128)(2,1)}, u32[]{:S(2)}) copy-start(bf16[4,64,1024]{2,1,0:T(8,128)(2,1)} %slice.149) | copy-start | bytes 1572868
  90.0 19.8 %all-to-all-start = ((bf16[4,48,1024]{2,1,0:T(8,128)(2,1)}), bf16[4,48,1024]{2,1,0:T(8,128)(2,1)S(1)}, u32[]{:S(2)}, u32[]{:S(2)}) async-start(bf16[4,48,1024]{2,1,0:T(8,128)(2,1)} %bitcast.171), calls=%async_computation.1 | async-start | bytes 786432 | tf_op jit(solution)/shard_map/all_to_all | solution.py:18
  112.1 10.3 %all-to-all-start.3 = ((bf16[4,48,256]{2,1,0:T(8,128)(2,1)}), bf16[4,48,256]{2,1,0:T(8,128)(2,1)S(1)}, u32[]{:S(2)}, u32[]{:S(2)}) async-start(bf16[4,48,256]{2,1,0:T(8,128)(2,1)} %bitcast.28), calls=%async_computation.4 | async-start | bytes 196608 | tf_op jit(solution)/shard_map/all_to_all | solution.py:18
  124.0 23.0 %all-to-all-start.4 = ((bf16[8,88,128]{2,1,0:T(8,128)(2,1)}), bf16[8,88,128]{2,1,0:T(8,128)(2,1)S(1)}, u32[]{:S(2)}, u32[]{:S(2)}) async-start(bf16[8,88,128]{2,1,0:T(8,128)(2,1)} %broadcast_in_dim.120), calls=%async_computation.5 | async-start | bytes 360448 | tf_op jit(solution)/shard_map/all_to_all | solution.py:18
  130.0 17.4 %copy-start.9 = (bf16[48,128]{1,0:T(8,128)(2,1)S(1)}, bf16[48,128]{1,0:T(8,128)(2,1)}, u32[]{:S(2)}) copy-start(bf16[48,128]{1,0:T(8,128)(2,1)} %copy-done.8) | copy-start | bytes 36868
  130.1 18.3 %copy-start.2 = (bf16[38,8,8,128]{3,2,0,1:T(8,128)(2,1)}, bf16[38,8,8,128]{3,2,0,1:T(8,128)(2,1)S(1)}, u32[]{:S(2)}) copy-start(bf16[38,8,8,128]{3,2,0,1:T(8,128)(2,1)S(1)} %copy.242) | copy-start | bytes 1867780
  149.3 21.3 %all-to-all-start.5 = ((bf16[4,80,1024]{2,1,0:T(8,128)(2,1)}), bf16[4,80,1024]{2,1,0:T(8,128)(2,1)S(1)}, u32[]{:S(2)}, u32[]{:S(2)}) async-start(bf16[4,80,1024]{2,1,0:T(8,128)(2,1)} %pad_maximum_fusion.2), calls=%async_computation.6 | async-start | bytes 1310720 | tf_op jit(solution)/shard_map/all_to_all | solution.py:18
  153.0 49.0 %reduce-scatter.5.cloned.1.call-start = ((), (), s32[]{:S(2)}) async-start(), calls=%async_computation.12 | async-start | bytes 700416 | tf_op jit(solution)/shard_map/reduce_scatter | solution.py:176
  153.7 61.8 %all-gather.5.cloned.1.call-start = ((), (), s32[]{:S(2)}) async-start(), calls=%async_computation.13 | async-start | bytes 2949120 | tf_op jit(solution)/shard_map/all_gather | solution.py:67
  173.2 29.9 %copy-start.14 = (pred[96]{0:T(512)(128)(4,1)S(1)}, pred[96]{0:T(512)(128)(4,1)}, u32[]{:S(2)}) copy-start(pred[96]{0:T(512)(128)(4,1)} %get-tuple-element.37) | copy-start | bytes 292
  173.2 31.1 %all-to-all-start.6 = ((bf16[16,200,256]{2,1,0:T(8,128)(2,1)}), bf16[16,200,256]{2,1,0:T(8,128)(2,1)S(1)}, u32[]{:S(2)}, u32[]{:S(2)}) async-start(bf16[16,200,256]{2,1,0:T(8,128)(2,1)} %maximum_maximum_fusion), calls=%async_computation.7 | async-start | bytes 3276800 | tf_op jit(solution)/shard_map/all_to_all | solution.py:18
  205.2 29.1 %all-to-all-start.7 = ((bf16[64,15,128]{2,1,0:T(8,128)(2,1)}), bf16[64,15,128]{2,1,0:T(8,128)(2,1)S(1)}, u32[]{:S(2)}, u32[]{:S(2)}) async-start(bf16[64,15,128]{2,1,0:T(8,128)(2,1)} %pad_maximum_fusion.4), calls=%async_computation.9 | async-start | bytes 524288 | tf_op jit(solution)/shard_map/all_to_all | solution.py:18
Sparse Core Ops, SparseCore 0:
  36.4 33.1 reduce-scatter.2
  156.6 45.2 reduce-scatter.4
Sparse Core Ops, SparseCore 1:
  90.1 34.2 all-gather.2
  156.3 50.3 all-gather.4
where the time goes:
time: 245 us; the launch traced here: 244 us
  blocking collectives  75.6 us (31%)
  waiting for transfers between devices  66.2 us (27%)
  starting transfers between devices  49.3 us (20%)
  between operations  18.4 us (8%)
  local copies, waits for them, and re-layouts  13.3 us (5%)
  matrix products  13.2 us (5%)
  other arithmetic  8.08 us (3%)
    all_to_all x7, waiting for transfers between devices, exchange(): return lax.all_to_all(blocks, axis, split_axis=0, concat_axis=0, tiled=True)  42 us
    all_to_all x7, starting transfers between devices, exchange(): return lax.all_to_all(blocks, axis, split_axis=0, concat_axis=0, tiled=True)  38.2 us
    all_to_all x1, blocking collectives, exchange(): return lax.all_to_all(blocks, axis, split_axis=0, concat_axis=0, tiled=True)  35.7 us
    reduce_scatter x1, waiting for transfers between devices, shards(): summed = lax.psum_scatter(base, TP, scatter_dimension=0, tiled=True)  22.8 us
    all_gather x1, blocking collectives, shards(): lax.all_gather(projector_grad, 'y', axis=1, tiled=True).astype(f32)  14.4 us
    all_gather x1, blocking collectives, shards(): grad_all = lax.all_gather(grad_full, 'y', axis=0, tiled=True)  13.7 us
    dot_general x17, matrix products, dot(): lax.dot_general(a, b, (((ca,), (cb,)), ((), ())), preferred_element_type=...  13.2 us
    all_gather x1, blocking collectives, shards(): weights = lax.all_gather(weights, 'x')  11.8 us
  transfers between devices with their start and end apart: 14, of which 6 were waited for; matrix products, arithmetic and copies ran while one was open for 11% of the time, Pallas kernels for 0%

commit v1 on v0

--- a/solution.py
+++ b/solution.py
@@ -207,7 +207,9 @@
     up_grad = last[:, n_d].astype(f32)
     all_grad = came[:, :n_x].reshape(ny * nx * n_x, quarter)
     projector_grad = after(dot(all_frames, all_grad, 0, 0), summed).astype(bf16)
-    projector_grad = lax.all_gather(projector_grad, "y", axis=1, tiled=True).astype(f32)
+    projector_grad = jnp.concatenate(
+        lax.all_to_all(jnp.stack([projector_grad] * lax.axis_size("y"), axis=0), "y", 0, 0), axis=1
+    ).astype(f32)
     in_slots = last[:, -cap:].reshape(nzl, ny, nx * cap, cols)
     in_slots = lax.dynamic_index_in_dim(in_slots, y_index, 1, False).reshape(slots, cols)
     audio_values = dot(receiver, in_slots, 1, 0).astype(bf16)

time: 245 us -> 257 us (1.049)
  waiting for transfers between devices: 66.2 us -> 84.2 us
  blocking collectives: 75.6 us -> 62.3 us
  starting transfers between devices: 49.3 us -> 53.9 us
  local copies, waits for them, and re-layouts: 13.3 us -> 17 us
    all_to_all x7, waiting for transfers between devices: 42 us -> 75 us  [exchange(): return lax.all_to_all(blocks, axis, split_axis=0, concat_axis=0, tiled=True)]
    reduce_scatter x1, waiting for transfers between devices: 22.8 us -> 0.01 us  [shards(): summed = lax.psum_scatter(base, TP, scatter_dimension=0, tiled=True)]
    all_gather x1 -> x0, blocking collectives: 14.4 us -> none  [shards(): lax.all_gather(projector_grad, 'y', axis=1, tiled=True).astype(f32)]
    all_to_all x0 -> x1, waiting for transfers between devices: none -> 8.52 us  [shards(): lax.all_to_all(jnp.stack([projector_grad] * lax.axis_size('y'), axis=0),...]
    all_to_all x0 -> x1, starting transfers between devices: none -> 3.48 us  [shards(): lax.all_to_all(jnp.stack([projector_grad] * lax.axis_size('y'), axis=0),...]
  transfers between devices with their start and end apart: 14 -> 15, of which waited for: 6 -> 7; matrix products, arithmetic and copies ran while one was open for 11% -> 11% of each run, Pallas kernels for 0% -> 0%
where the time goes in v1:
time: 257 us; the launch traced here: 256 us
  waiting for transfers between devices  84.2 us (33%)
  blocking collectives  62.3 us (24%)
  starting transfers between devices  53.9 us (21%)
  between operations  18.3 us (7%)
  local copies, waits for them, and re-layouts  17 us (7%)
  matrix products  13.2 us (5%)
  other arithmetic  7.13 us (3%)
    all_to_all x7, waiting for transfers between devices, exchange(): return lax.all_to_all(blocks, axis, split_axis=0, concat_axis=0, tiled=True)  75 us
    all_to_all x7, starting transfers between devices, exchange(): return lax.all_to_all(blocks, axis, split_axis=0, concat_axis=0, tiled=True)  39.4 us
    all_to_all x1, blocking collectives, exchange(): return lax.all_to_all(blocks, axis, split_axis=0, concat_axis=0, tiled=True)  35.7 us
    all_gather x1, blocking collectives, shards(): grad_all = lax.all_gather(grad_full, 'y', axis=0, tiled=True)  13.7 us
    dot_general x17, matrix products, dot(): lax.dot_general(a, b, (((ca,), (cb,)), ((), ())), preferred_element_type=...  13.2 us
    all_gather x1, blocking collectives, shards(): weights = lax.all_gather(weights, 'x')  12.9 us
    ppermute x3, starting transfers between devices, shards(): lax.ppermute(for_y(k), 'y', [(i, (i + k) % ny) for i in range(ny)])  10.9 us
    all_to_all x1, waiting for transfers between devices, shards(): lax.all_to_all(jnp.stack([projector_grad] * lax.axis_size('y'), axis=0),...  8.52 us
  transfers between devices with their start and end apart: 15, of which 7 were waited for; matrix products, arithmetic and copies ran while one was open for 11% of the time, Pallas kernels for 0%

profile of v1, /device:TPU:2, one launch (start us, length us, event | category | flops | bytes accessed | tf_op | source)
XLA Modules:
  0.0 256.1 jit_solution(13364328456596634284)
XLA Ops:
  8.1 1.1 dynamic-slice_bitcast_fusion
  9.2 0.8 constant_dynamic-slice_fusion.6
  10.1 0.7 pad_maximum_fusion.6
  10.8 5.1 %collective-permute-start.1 = (bf16[640,128]{1,0:T(8,128)(2,1)}, bf16[640,128]{1,0:T(8,128)(2,1)S(1)}, u32[]{:S(2)}, u32[]{:S(2)}) collective-permute-start(bf16[640,128]{1,0:T(8,128)(2,1)} %get-tuple-element.21), channel_id=1, source_target_pairs={{0,16},{8,24},{16,0},{24,8},{1,17},{9,25},{17,1},{25,9},{2,18},{10... | collective-permute-start | bytes 491528 | tf_op jit(solution)/shard_map/ppermute | solution.py:107
  15.9 3.0 %collective-permute-start.2 = (bf16[640,128]{1,0:T(8,128)(2,1)S(1)}, bf16[640,128]{1,0:T(8,128)(2,1)S(1)}, u32[]{:S(2)}, u32[]{:S(2)}) collective-permute-start(bf16[640,128]{1,0:T(8,128)(2,1)S(1)} %get-tuple-element.22), channel_id=1, source_target_pairs={{0,24},{8,0},{16,8},{24,16},{1,25},{9,1},{17,9},{25,17},{2,26},{10... | collective-permute-start | bytes 491528 | tf_op jit(solution)/shard_map/ppermute | solution.py:107
  18.9 2.9 %collective-permute-start = (bf16[640,128]{1,0:T(8,128)(2,1)S(1)}, bf16[640,128]{1,0:T(8,128)(2,1)S(1)}, u32[]{:S(2)}, u32[]{:S(2)}) collective-permute-start(bf16[640,128]{1,0:T(8,128)(2,1)S(1)} %get-tuple-element.20), channel_id=1, source_target_pairs={{0,8},{8,16},{16,24},{24,0},{1,9},{9,17},{17,25},{25,1},{2,10},{10... | collective-permute-start | bytes 491528 | tf_op jit(solution)/shard_map/ppermute | solution.py:107
  23.3 0.6 reshape.410
  24.0 8.9 %all-to-all-start.1 = ((bf16[16,6,128]{2,1,0:T(8,128)(2,1)}), bf16[16,6,128]{2,1,0:T(8,128)(2,1)S(1)}, u32[]{:S(2)}, u32[]{:S(2)}) async-start(bf16[16,6,128]{2,1,0:T(8,128)(2,1)} %reshape.410), calls=%async_computation.2 | async-start | bytes 65536 | tf_op jit(solution)/shard_map/all_to_all | solution.py:18
  33.3 2.1 convolution_convert_fusion
  36.3 0.7 dynamic_slice.32
  37.1 2.5 all-to-all-done.1
  40.4 0.9 copy-done.3
  41.8 35.7 %all_to_all.45 = bf16[8,160,128]{2,1,0:T(8,128)(2,1)S(1)} all-to-all(bf16[8,160,128]{2,1,0:T(8,128)(2,1)S(1)} %pad_maximum_fusion.3), channel_id=1, replica_groups=mesh['zl'=4,'x'=4,'y'=4,'zh'=4,'c'=2] {'zh','c'}, dimensions={0} | all-to-all | bytes 655360 | tf_op jit(solution)/shard_map/all_to_all | solution.py:18
  77.6 12.9 %all_gather.13 = bf16[4,80,1024]{2,1,0:T(8,128)(2,1)S(1)} all-gather(bf16[1,80,1024]{2,1,0:T(8,128)(2,1)S(1)} %all_gather_reshape.3), channel_id=1, replica_groups=mesh['zl'=4,'x'=4,'y'=4,'zh'=4,'c'=2] {'x'}, dimensions={0}, use_global_device_ids=true | all-gather | bytes 819200 | tf_op jit(solution)/shard_map/all_gather | solution.py:143
  90.6 0.8 slice.149
  91.5 4.6 %all-to-all-start = ((bf16[4,48,1024]{2,1,0:T(8,128)(2,1)}), bf16[4,48,1024]{2,1,0:T(8,128)(2,1)S(1)}, u32[]{:S(2)}, u32[]{:S(2)}) async-start(bf16[4,48,1024]{2,1,0:T(8,128)(2,1)} %bitcast.176), calls=%async_computation.1 | async-start | bytes 786432 | tf_op jit(solution)/shard_map/all_to_all | solution.py:18
  96.3 13.7 %all_gather.12 = bf16[192,1024]{1,0:T(8,128)(2,1)S(1)} all-gather(bf16[48,1024]{1,0:T(8,128)(2,1)S(1)} %copy_bitcast_fusion.1), channel_id=1, replica_groups=mesh['zl'=4,'x'=4,'y'=4,'zh'=4,'c'=2] {'y'}, dimensions={0}, use_global_device_ids=true | all-gather | bytes 491520 | tf_op jit(solution)/shard_map/all_gather | solution.py:141
  110.3 0.5 slice.150
  111.5 1.0 fusion.5
  112.4 3.4 %all-to-all-start.3 = ((bf16[4,48,256]{2,1,0:T(8,128)(2,1)}), bf16[4,48,256]{2,1,0:T(8,128)(2,1)S(1)}, u32[]{:S(2)}, u32[]{:S(2)}) async-start(bf16[4,48,256]{2,1,0:T(8,128)(2,1)} %bitcast.28), calls=%async_computation.4 | async-start | bytes 196608 | tf_op jit(solution)/shard_map/all_to_all | solution.py:18
  116.0 6.7 %all-to-all-done.3 = bf16[4,48,256]{2,1,0:T(8,128)(2,1)S(1)} async-done(((bf16[4,48,256]{2,1,0:T(8,128)(2,1)}), bf16[4,48,256]{2,1,0:T(8,128)(2,1)S(1)}, u32[]{:S(2)}, u32[]{:S(2)}) %all-to-all-start.3) | async-done | bytes 98336 | tf_op jit(solution)/shard_map/all_to_all | solution.py:18
  123.6 0.7 broadcast_in_dim.120
  124.3 3.4 %all-to-all-start.4 = ((bf16[8,88,128]{2,1,0:T(8,128)(2,1)}), bf16[8,88,128]{2,1,0:T(8,128)(2,1)S(1)}, u32[]{:S(2)}, u32[]{:S(2)}) async-start(bf16[8,88,128]{2,1,0:T(8,128)(2,1)} %broadcast_in_dim.120), calls=%async_computation.5 | async-start | bytes 360448 | tf_op jit(solution)/shard_map/all_to_all | solution.py:18
  127.9 2.4 fusion
  130.3 0.9 copy.273
  131.3 1.2 slice.158
  133.2 14.2 %all-to-all-done.4 = bf16[8,88,128]{2,1,0:T(8,128)(2,1)S(1)} async-done(((bf16[8,88,128]{2,1,0:T(8,128)(2,1)}), bf16[8,88,128]{2,1,0:T(8,128)(2,1)S(1)}, u32[]{:S(2)}, u32[]{:S(2)}) %all-to-all-start.4) | async-done | bytes 180256 | tf_op jit(solution)/shard_map/all_to_all | solution.py:18
  148.7 0.9 pad_maximum_fusion.2
  149.6 3.6 %all-to-all-start.5 = ((bf16[4,80,1024]{2,1,0:T(8,128)(2,1)}), bf16[4,80,1024]{2,1,0:T(8,128)(2,1)S(1)}, u32[]{:S(2)}, u32[]{:S(2)}) async-start(bf16[4,80,1024]{2,1,0:T(8,128)(2,1)} %pad_maximum_fusion.2), calls=%async_computation.6 | async-start | bytes 1310720 | tf_op jit(solution)/shard_map/all_to_all | solution.py:18
  153.3 0.6 all-gather.5.cloned.1.call-update
  153.9 23.1 %all-to-all-done.5 = bf16[4,80,1024]{2,1,0:T(8,128)(2,1)S(1)} async-done(((bf16[4,80,1024]{2,1,0:T(8,128)(2,1)}), bf16[4,80,1024]{2,1,0:T(8,128)(2,1)S(1)}, u32[]{:S(2)}, u32[]{:S(2)}) %all-to-all-start.5) | async-done | bytes 655392 | tf_op jit(solution)/shard_map/all_to_all | solution.py:18
  177.6 1.8 maximum_maximum_fusion
  179.5 5.1 %all-to-all-start.6 = ((bf16[16,200,256]{2,1,0:T(8,128)(2,1)}), bf16[16,200,256]{2,1,0:T(8,128)(2,1)S(1)}, u32[]{:S(2)}, u32[]{:S(2)}) async-start(bf16[16,200,256]{2,1,0:T(8,128)(2,1)} %maximum_maximum_fusion), calls=%async_computation.7 | async-start | bytes 3276800 | tf_op jit(solution)/shard_map/all_to_all | solution.py:18
  184.6 1.2 slice.176
  186.4 1.1 fusion.4
  187.6 18.9 %all-to-all-done.6 = bf16[16,200,256]{2,1,0:T(8,128)(2,1)S(1)} async-done(((bf16[16,200,256]{2,1,0:T(8,128)(2,1)}), bf16[16,200,256]{2,1,0:T(8,128)(2,1)S(1)}, u32[]{:S(2)}, u32[]{:S(2)}) %all-to-all-start.6) | async-done | bytes 1638432 | tf_op jit(solution)/shard_map/all_to_all | solution.py:18
  206.4 1.3 slice.175
  207.7 3.1 %fusion.2 = bf16[320,256]{1,0:T(8,128)(2,1)S(1)} fusion(bf16[3072,256]{1,0:T(8,128)(2,1)} %bitcast.162, bf16[3072,320]{1,0:T(8,128)(2,1)} %all-gather.5.cloned.1.call-done, f32[]{:T(128)S(6)} %convert.14), kind=kOutput, calls=%fused_computation.13 | convolution fusion | flops 503480320 | bytes 3702788 | tf_op jit(solution)/shard_map/dot_general | solution.py:14
  210.9 0.9 stack.27
  211.8 3.5 %all-to-all-start.8 = ((bf16[4,320,256]{2,1,0:T(8,128)(2,1)}), bf16[4,320,256]{2,1,0:T(8,128)(2,1)S(1)}, u32[]{:S(2)}, u32[]{:S(2)}) async-start(bf16[4,320,256]{2,1,0:T(8,128)(2,1)} %stack.27), calls=%async_computation.10 | async-start | bytes 1310720 | tf_op jit(solution)/shard_map/all_to_all | solution.py:211
  215.7 0.8 pad_maximum_fusion.4
  216.4 8.5 %all-to-all-done.8 = bf16[4,320,256]{2,1,0:T(8,128)(2,1)S(1)} async-done(((bf16[4,320,256]{2,1,0:T(8,128)(2,1)}), bf16[4,320,256]{2,1,0:T(8,128)(2,1)S(1)}, u32[]{:S(2)}, u32[]{:S(2)}) %all-to-all-start.8) | async-done | bytes 655392 | tf_op jit(solution)/shard_map/all_to_all | solution.py:211
  225.0 10.4 %all-to-all-start.7 = ((bf16[64,15,128]{2,1,0:T(8,128)(2,1)}), bf16[64,15,128]{2,1,0:T(8,128)(2,1)S(1)}, u32[]{:S(2)}, u32[]{:S(2)}) async-start(bf16[64,15,128]{2,1,0:T(8,128)(2,1)} %pad_maximum_fusion.4), calls=%async_computation.9 | async-start | bytes 524288 | tf_op jit(solution)/shard_map/all_to_all | solution.py:18
  235.5 1.2 copy.250
  236.7 9.6 %all-to-all-done.7 = bf16[64,15,128]{2,1,0:T(8,128)(2,1)S(1)} async-done(((bf16[64,15,128]{2,1,0:T(8,128)(2,1)}), bf16[64,15,128]{2,1,0:T(8,128)(2,1)S(1)}, u32[]{:S(2)}, u32[]{:S(2)}) %all-to-all-start.7) | async-done | bytes 245792 | tf_op jit(solution)/shard_map/all_to_all | solution.py:18
  246.5 0.8 copy.274
  247.2 0.9 fusion.6
  248.1 0.6 slice_convert_fusion.2
  (148 shorter events, 8.6 us)
Async XLA Ops:
  8.0 25.3 %copy-start = (bf16[320,1024]{1,0:T(8,128)(2,1)S(1)}, bf16[320,1024]{1,0:T(8,128)(2,1)}, u32[]{:S(2)}) copy-start(bf16[320,1024]{1,0:T(8,128)(2,1)} %param.13) | copy-start | bytes 1966084
  8.0 13.8 %copy-start.7 = (s32[1,16,16]{2,1,0:T(8,128)S(1)}, s32[1,16,16]{2,1,0:T(8,128)}, u32[]{:S(2)}) copy-start(s32[1,16,16]{2,1,0:T(8,128)} %param.19) | copy-start | bytes 3076
  8.0 13.8 %copy-start.8 = (s32[1,16,16]{2,1,0:T(8,128)S(1)}, s32[1,16,16]{2,1,0:T(8,128)}, u32[]{:S(2)}) copy-start(s32[1,16,16]{2,1,0:T(8,128)} %param.20) | copy-start | bytes 3076
  8.0 14.8 %copy-start.9 = (s32[256]{0:T(256)S(1)}, s32[256]{0:T(256)}, u32[]{:S(2)}) copy-start(s32[256]{0:T(256)} %param.22) | copy-start | bytes 3076
  8.0 14.8 %copy-start.10 = (s32[256]{0:T(256)S(1)}, s32[256]{0:T(256)}, u32[]{:S(2)}) copy-start(s32[256]{0:T(256)} %param.21) | copy-start | bytes 3076
  8.1 15.0 %copy-start.5 = (bf16[256,128]{1,0:T(8,128)(2,1)S(1)}, bf16[256,128]{1,0:T(8,128)(2,1)}, u32[]{:S(2)}) copy-start(bf16[256,128]{1,0:T(8,128)(2,1)} %param.23) | copy-start | bytes 196612
  8.1 24.8 %copy-start.4 = (bf16[768,320]{0,1:T(8,128)(2,1)S(1)}, bf16[768,320]{0,1:T(8,128)(2,1)}, u32[]{:S(2)}) copy-start(bf16[768,320]{0,1:T(8,128)(2,1)} %param.12) | copy-start | bytes 1474564
  10.8 29.1 %collective-permute-start.1 = (bf16[640,128]{1,0:T(8,128)(2,1)}, bf16[640,128]{1,0:T(8,128)(2,1)S(1)}, u32[]{:S(2)}, u32[]{:S(2)}) collective-permute-start(bf16[640,128]{1,0:T(8,128)(2,1)} %get-tuple-element.21), channel_id=1, source_target_pairs={{0,16},{8,24},{16,0},{24,8},{1,17},{9,25},{17,1},{25,9},{2,18},{10... | collective-permute-start | bytes 491528 | tf_op jit(solution)/shard_map/ppermute | solution.py:107
  15.9 24.0 %collective-permute-start.2 = (bf16[640,128]{1,0:T(8,128)(2,1)S(1)}, bf16[640,128]{1,0:T(8,128)(2,1)S(1)}, u32[]{:S(2)}, u32[]{:S(2)}) collective-permute-start(bf16[640,128]{1,0:T(8,128)(2,1)S(1)} %get-tuple-element.22), channel_id=1, source_target_pairs={{0,24},{8,0},{16,8},{24,16},{1,25},{9,1},{17,9},{25,17},{2,26},{10... | collective-permute-start | bytes 491528 | tf_op jit(solution)/shard_map/ppermute | solution.py:107
  18.9 21.1 %collective-permute-start = (bf16[640,128]{1,0:T(8,128)(2,1)S(1)}, bf16[640,128]{1,0:T(8,128)(2,1)S(1)}, u32[]{:S(2)}, u32[]{:S(2)}) collective-permute-start(bf16[640,128]{1,0:T(8,128)(2,1)S(1)} %get-tuple-element.20), channel_id=1, source_target_pairs={{0,8},{8,16},{16,24},{24,0},{1,9},{9,17},{17,25},{25,1},{2,10},{10... | collective-permute-start | bytes 491528 | tf_op jit(solution)/shard_map/ppermute | solution.py:107
  24.0 15.7 %all-to-all-start.1 = ((bf16[16,6,128]{2,1,0:T(8,128)(2,1)}), bf16[16,6,128]{2,1,0:T(8,128)(2,1)S(1)}, u32[]{:S(2)}, u32[]{:S(2)}) async-start(bf16[16,6,128]{2,1,0:T(8,128)(2,1)} %reshape.410), calls=%async_computation.2 | async-start | bytes 65536 | tf_op jit(solution)/shard_map/all_to_all | solution.py:18
  32.9 58.6 %reduce-scatter.3.cloned.1.call-start = ((), (), s32[]{:S(2)}) async-start(), calls=%async_computation.11 | async-start | bytes 1966080 | tf_op jit(solution)/shard_map/reduce_scatter | solution.py:66
  33.3 2.2 copy-start.2
  35.4 1.5 copy-start.6
  35.5 92.5 %all-gather.3.cloned.1.call-start = ((), (), s32[]{:S(2)}) async-start(), calls=%async_computation.12 | async-start | bytes 2621440 | tf_op jit(solution)/shard_map/all_gather | solution.py:151
  40.2 1.0 copy-start.3
  91.4 20.0 %copy-start.1 = (bf16[4,64,1024]{2,1,0:T(8,128)(2,1)S(1)}, bf16[4,64,1024]{2,1,0:T(8,128)(2,1)}, u32[]{:S(2)}) copy-start(bf16[4,64,1024]{2,1,0:T(8,128)(2,1)} %slice.149) | copy-start | bytes 1572868
  91.5 18.7 %all-to-all-start = ((bf16[4,48,1024]{2,1,0:T(8,128)(2,1)}), bf16[4,48,1024]{2,1,0:T(8,128)(2,1)S(1)}, u32[]{:S(2)}, u32[]{:S(2)}) async-start(bf16[4,48,1024]{2,1,0:T(8,128)(2,1)} %bitcast.176), calls=%async_computation.1 | async-start | bytes 786432 | tf_op jit(solution)/shard_map/all_to_all | solution.py:18
  112.4 10.3 %all-to-all-start.3 = ((bf16[4,48,256]{2,1,0:T(8,128)(2,1)}), bf16[4,48,256]{2,1,0:T(8,128)(2,1)S(1)}, u32[]{:S(2)}, u32[]{:S(2)}) async-start(bf16[4,48,256]{2,1,0:T(8,128)(2,1)} %bitcast.28), calls=%async_computation.4 | async-start | bytes 196608 | tf_op jit(solution)/shard_map/all_to_all | solution.py:18
  124.3 23.0 %all-to-all-start.4 = ((bf16[8,88,128]{2,1,0:T(8,128)(2,1)}), bf16[8,88,128]{2,1,0:T(8,128)(2,1)S(1)}, u32[]{:S(2)}, u32[]{:S(2)}) async-start(bf16[8,88,128]{2,1,0:T(8,128)(2,1)} %broadcast_in_dim.120), calls=%async_computation.5 | async-start | bytes 360448 | tf_op jit(solution)/shard_map/all_to_all | solution.py:18
  127.7 56.9 %reduce-scatter.5.cloned.1.call-start = ((), (), s32[]{:S(2)}) async-start(), calls=%async_computation.13 | async-start | bytes 700416 | tf_op jit(solution)/shard_map/reduce_scatter | solution.py:176
  149.6 27.4 %all-to-all-start.5 = ((bf16[4,80,1024]{2,1,0:T(8,128)(2,1)}), bf16[4,80,1024]{2,1,0:T(8,128)(2,1)S(1)}, u32[]{:S(2)}, u32[]{:S(2)}) async-start(bf16[4,80,1024]{2,1,0:T(8,128)(2,1)} %pad_maximum_fusion.2), calls=%async_computation.6 | async-start | bytes 1310720 | tf_op jit(solution)/shard_map/all_to_all | solution.py:18
  153.3 54.5 %all-gather.5.cloned.1.call-start = ((), (), s32[]{:S(2)}) async-start(), calls=%async_computation.14 | async-start | bytes 2949120 | tf_op jit(solution)/shard_map/all_gather | solution.py:67
  179.5 27.0 %all-to-all-start.6 = ((bf16[16,200,256]{2,1,0:T(8,128)(2,1)}), bf16[16,200,256]{2,1,0:T(8,128)(2,1)S(1)}, u32[]{:S(2)}, u32[]{:S(2)}) async-start(bf16[16,200,256]{2,1,0:T(8,128)(2,1)} %maximum_maximum_fusion), calls=%async_computation.7 | async-start | bytes 3276800 | tf_op jit(solution)/shard_map/all_to_all | solution.py:18
  211.8 13.2 %all-to-all-start.8 = ((bf16[4,320,256]{2,1,0:T(8,128)(2,1)}), bf16[4,320,256]{2,1,0:T(8,128)(2,1)S(1)}, u32[]{:S(2)}, u32[]{:S(2)}) async-start(bf16[4,320,256]{2,1,0:T(8,128)(2,1)} %stack.27), calls=%async_computation.10 | async-start | bytes 1310720 | tf_op jit(solution)/shard_map/all_to_all | solution.py:211
  225.0 21.4 %all-to-all-start.7 = ((bf16[64,15,128]{2,1,0:T(8,128)(2,1)}), bf16[64,15,128]{2,1,0:T(8,128)(2,1)S(1)}, u32[]{:S(2)}, u32[]{:S(2)}) async-start(bf16[64,15,128]{2,1,0:T(8,128)(2,1)} %pad_maximum_fusion.4), calls=%async_computation.9 | async-start | bytes 524288 | tf_op jit(solution)/shard_map/all_to_all | solution.py:18
Sparse Core Ops, SparseCore 0:
  36.5 33.2 reduce-scatter.2
  131.4 52.1 reduce-scatter.4
Sparse Core Ops, SparseCore 1:
  91.5 33.1 all-gather.2
  155.8 37.1 all-gather.4
